TPU v7x, 32 devices: a whole 2x2x4 slice. The times are simulated.
32 devices in a mesh: row: 4 (over y, x), tile: 8 (over z, core).
Axes of the slice: x: 2, y: 2, z: 4, core: 2. Of those that a mesh axis runs over, the one named last changes fastest.
Arguments:
- row_points: float32 [3, 16384], replicated, may hold values from 0 to 6, as said below
- source_points: float32 [3, 32768], P(None, 'tile'), may hold values from -2.5 to 6, as said below
- sketch: bfloat16 [32768, 128], P('tile'), may hold values from -6 to 6
- admissible: int32 [4, 256], P('row', 'tile'), may hold values from 0 to 1, as said below
Outputs:
- basis: float32 [16384, 128], P(('row', 'tile'))
- projected: bfloat16 [4, 128, 32768], P('row', None, 'tile')
Inputs may be any that keep to these rules, and one draw needn't show every extreme that they name: In every block row, the 32 panels of some index of tile are all admissible; how many panels of an index of tile are admissible varies widely. `row_points`: the first two coordinates lie in 0 to 6 and the third in 0 to 0.25. `source_points`: the first two coordinates lie in 0 to 6 and the third in -2.5 to -0.5.
All inputs are finite; a program needn't handle non-finite values.
Results may differ from a plain program's by a relative error of at most 0.0055.
Values may be sent and summed in bfloat16 or wider, within the bound.
No kernel may reach another device: no remote copies, remote signals or barrier semaphores. Data moves between devices by JAX's collectives and lax.ppermute only.
A program may use at most 64 MiB of HBM per device.

v0:
```python
import functools
import math

import jax
import jax.numpy as jnp
from jax import lax
from jax.experimental import pallas as pl
from jax.experimental.pallas import tpu as pltpu
from jax.sharding import PartitionSpec as P

DAMPING = 0.25
WAVENUM = 24.0
SHIFT = 0.0001

TURNS = WAVENUM / (2.0 * math.pi)
DECAY = -DAMPING / TURNS / math.log(2.0)
AMP = TURNS / (4.0 * math.pi)
S0, S1, S2 = 6.28127979 * AMP, -41.0952178 * AMP, 73.5851113 * AMP

WIDTH = 128
PAIR = 2 * WIDTH
TERMS = 32
SUB = 8
PIECE = 16
GROUP = 4
WHOLE = 1.5 * 2.0**23


def head(x):
    return x.astype(jnp.bfloat16).astype(jnp.float32)


def three(x):
    a = head(x)
    b = head(x - a)
    return a, b, x - a - b


def fill_terms(ref, points, side):
    at = lax.broadcasted_iota(jnp.int32, points.shape, 0)
    x = points - jnp.where(at == 2, -0.5, 3.0)
    scale = TURNS * TURNS
    norm = three(scale * jnp.sum(x * x, axis=0, keepdims=True))
    one = jnp.ones_like(norm[0])
    if side == 0:
        h, m, l = three(x)
        rows = [h, h, m, h, l, m]
        tail = [*norm, one, one, one]
    else:
        h, m, l = three(x * (-2.0 * scale))
        rows = [h, m, h, l, h, m]
        tail = [one, one, one, *norm]
    ref[...] = jnp.zeros_like(ref)
    for at, row in enumerate(rows):
        ref[3 * at : 3 * at + 3, :] = row
    for at, row in enumerate(tail):
        ref[18 + at : 19 + at, :] = row


def near_field(square):
    inv = lax.rsqrt(square)
    t = square * inv
    f = t - ((t + WHOLE) - WHOLE)
    g = 0.25 - jnp.abs(f)
    v = g * g
    wave = ((S2 * v + S1) * v + S0) * g
    amp = jnp.exp2(DECAY * t) * inv
    return (wave * amp).astype(jnp.bfloat16)


def order_panels(flags_ref, order_ref, panels):
    def step(p, count):
        @pl.when(flags_ref[0, p] > 0)
        def _():
            order_ref[count] = p

        return count + (flags_ref[0, p] > 0).astype(jnp.int32)

    count = lax.fori_loop(0, panels, step, jnp.int32(0))
    order_ref[panels] = count
    return count


def prep_kernel(
    flags_hbm, rows_hbm, src_hbm, omega_hbm, order_ref, src_pick, omega_pick, row_mat,
    flags, points, picked, row_terms, src_terms, sources, sems, sem, *, slices, place
):
    panels = flags.shape[1]
    rows = points.shape[1]
    me = lax.axis_index("tile")
    at = pl.multiple_of(lax.axis_index("row") * rows, rows) if place else 0
    copies = [
        pltpu.make_async_copy(flags_hbm, flags, sems.at[0]),
        pltpu.make_async_copy(rows_hbm.at[:, pl.ds(at, rows)], points, sems.at[1]),
        pltpu.make_async_copy(src_hbm, sources, sems.at[2]),
    ]
    for copy in copies:
        copy.start()
    copies[0].wait()
    count = order_panels(flags, order_ref, panels)

    def fetch(slot):
        at = pl.multiple_of(order_ref[slot] * WIDTH, WIDTH)
        to = pl.multiple_of(slot * WIDTH, WIDTH)
        return pltpu.make_async_copy(
            omega_hbm.at[pl.ds(at, WIDTH), :], omega_pick.at[pl.ds(to, WIDTH), :], sem
        )

    def start(slot, carry):
        fetch(slot).start()
        return carry

    lax.fori_loop(0, count, start, 0)
    copies[1].wait()
    if place:
        to = 0
        for k, first, size in slices:
            at = pl.multiple_of((me ^ k) * (rows // lax.axis_size("tile")) + first, WIDTH)
            picked[:, to : to + size] = points[:, pl.ds(at, size)]
            to += size
        fill_terms(row_terms, picked[...], 0)
    else:
        fill_terms(row_terms, points[...], 0)
    step = min(512, rows)
    for r in range(0, rows, step):
        row_mat[r : r + step, :] = row_terms[:, r : r + step].T.astype(jnp.bfloat16)
    copies[2].wait()
    fill_terms(src_terms, sources[...], 1)

    def pick(slot, carry):
        at = pl.multiple_of(order_ref[slot] * WIDTH, WIDTH)
        to = pl.multiple_of(slot * WIDTH, WIDTH)
        src_pick[:, pl.ds(to, WIDTH)] = src_terms[:, pl.ds(at, WIDTH)].astype(jnp.bfloat16)
        return carry

    lax.fori_loop(0, count, pick, 0)
    spare = src_terms[:, :WIDTH].astype(jnp.bfloat16)

    def pad(slot, carry):
        to = pl.multiple_of(slot * WIDTH, WIDTH)
        src_pick[:, pl.ds(to, WIDTH)] = spare
        omega_pick[pl.ds(to, WIDTH), :] = jnp.zeros((WIDTH, omega_pick.shape[1]), jnp.bfloat16)
        return carry

    lax.fori_loop(count, GROUP * ((count + GROUP - 1) // GROUP + 1), pad, 0)

    def finish(slot, carry):
        fetch(slot).wait()
        return carry

    lax.fori_loop(0, count, finish, 0)


def in_hbm(x):
    return pltpu.with_memory_space_constraint(x, pltpu.HBM)


def prep(admissible, points, source_points, sketch, rows, slices, place):
    panels = admissible.shape[1]
    cols, rank = sketch.shape
    spare = cols + 2 * GROUP * WIDTH
    hbm = pl.BlockSpec(memory_space=pltpu.HBM)
    vmem = pl.BlockSpec(memory_space=pltpu.VMEM)
    return pl.pallas_call(
        functools.partial(prep_kernel, slices=slices, place=place),
        in_specs=[hbm] * 4,
        out_specs=[pl.BlockSpec(memory_space=pltpu.SMEM), vmem, vmem, vmem],
        out_shape=[
            jax.ShapeDtypeStruct((panels + 8,), jnp.int32),
            jax.ShapeDtypeStruct((TERMS, spare), jnp.bfloat16),
            jax.ShapeDtypeStruct((spare, rank), jnp.bfloat16),
            jax.ShapeDtypeStruct((rows, TERMS), jnp.bfloat16),
        ],
        scratch_shapes=[
            pltpu.SMEM((1, panels), jnp.int32),
            pltpu.VMEM((3, rows), jnp.float32),
            pltpu.VMEM((3, rows), jnp.float32),
            pltpu.VMEM((TERMS, rows), jnp.float32),
            pltpu.VMEM((TERMS, cols), jnp.float32),
            pltpu.VMEM((3, cols), jnp.float32),
            pltpu.SemaphoreType.DMA((3,)),
            pltpu.SemaphoreType.DMA,
        ],
        compiler_params=pltpu.CompilerParams(vmem_limit_bytes=16 * 2**20),
        name="prep",
    )(*(in_hbm(x) for x in (admissible, points, source_points, sketch)))


def sketch_kernel(
    order_ref, src_pick, omega_pick, row_mat, part_ref, tiles_hbm, squares, tiles, total, sems,
    *, first, panels, rb
):
    groups = (order_ref[panels] + GROUP - 1) // GROUP
    cols = GROUP * WIDTH

    def block(b, carry):
        here = pl.ds(pl.multiple_of(b * rb, rb), rb)
        total[...] = jnp.zeros_like(total)
        tiles[1] = jnp.zeros(tiles.shape[1:], tiles.dtype)

        def columns(j):
            return pl.ds(pl.multiple_of(j * cols, cols), cols)

        def square_of(j):
            rows = row_mat[pl.ds(pl.multiple_of(first + b * rb, rb), rb), :]
            return jnp.dot(rows, src_pick[:, columns(j)], preferred_element_type=jnp.float32)

        def add(j, slot):
            tile = jnp.concatenate([tiles[slot, k] for k in range(GROUP)], axis=1)
            omega = omega_pick[columns(j), :]
            return total[...] + jnp.dot(tile, omega, preferred_element_type=jnp.float32)

        def keep(j):
            slot = lax.rem(j, 2)
            return pltpu.make_async_copy(
                tiles.at[slot], tiles_hbm.at[pl.ds(GROUP * j, GROUP), here, :], sems.at[slot]
            )

        squares[...] = square_of(0)

        def body(j, carry):
            @pl.when(j >= 2)
            def _():
                keep(j - 2).wait()

            slot = lax.rem(j, 2)
            square = squares[...]
            sums = add(jnp.maximum(j - 1, 0), 1 - slot)
            later = square_of(j + 1)
            near = [near_field(square[r : r + PIECE]) for r in range(0, rb, PIECE)]
            total[...] = sums
            squares[...] = later
            for r, piece in zip(range(0, rb, PIECE), near):
                for k in range(GROUP):
                    tiles[slot, k, r : r + PIECE, :] = piece[:, k * WIDTH : (k + 1) * WIDTH]
            keep(j).start()
            return carry

        lax.fori_loop(0, groups, body, 0)

        @pl.when(groups > 1)
        def _():
            keep(groups - 2).wait()

        @pl.when(groups > 0)
        def _():
            keep(groups - 1).wait()
            total[...] = add(groups - 1, lax.rem(groups - 1, 2))

        part_ref[here, :] = total[...]
        return carry

    lax.fori_loop(0, part_ref.shape[0] // rb, block, 0)


def sketch_pass(order, src_pick, omega_pick, row_mat, first, rows, panels):
    rank = omega_pick.shape[1]
    rb = min(512, rows)
    vmem = pl.BlockSpec(memory_space=pltpu.VMEM)
    return pl.pallas_call(
        functools.partial(sketch_kernel, first=first, panels=panels, rb=rb),
        in_specs=[pl.BlockSpec(memory_space=pltpu.SMEM), vmem, vmem, vmem],
        out_specs=[vmem, pl.BlockSpec(memory_space=pltpu.HBM)],
        out_shape=[
            jax.ShapeDtypeStruct((rows, rank), jnp.float32),
            pltpu.HBM((GROUP * ((panels + GROUP - 1) // GROUP), rows, WIDTH), jnp.bfloat16),
        ],
        scratch_shapes=[
            pltpu.VMEM((rb, GROUP * WIDTH), jnp.float32),
            pltpu.VMEM((2, GROUP, rb, WIDTH), jnp.bfloat16),
            pltpu.VMEM((rb, rank), jnp.float32),
            pltpu.SemaphoreType.DMA((2,)),
        ],
        compiler_params=pltpu.CompilerParams(vmem_limit_bytes=16 * 2**20),
        cost_estimate=pl.CostEstimate(
            flops=rows * panels * WIDTH * rank * 16, bytes_accessed=rows * panels * WIDTH * 2, transcendentals=0
        ),
        name="sketch_pass",
    )(order, src_pick, omega_pick, row_mat)


def pair_sum_kernel(own_ref, got_ref, kept_ref, *sent_refs):
    q = kept_ref.shape[0]
    for k in range(1 + len(sent_refs)):
        part = slice(k * q, (k + 1) * q)
        value = own_ref[part, :] + got_ref[part, :].astype(jnp.float32)
        if k == 0:
            kept_ref[...] = value
        else:
            sent_refs[k - 1][...] = value.astype(jnp.bfloat16)


def pair_sum(own, got, slots):
    q, rank = own.shape[0] // slots, own.shape[1]
    shapes = [jax.ShapeDtypeStruct((q, rank), jnp.float32)]
    shapes += [jax.ShapeDtypeStruct((q, rank), jnp.bfloat16)] * (slots - 1)
    return pl.pallas_call(pair_sum_kernel, out_shape=shapes, name="pair_sum")(own, got)


def row_sum_kernel(kept_ref, *refs):
    total = kept_ref[...]
    for ref in refs[:-1]:
        total = total + ref[...].astype(jnp.float32)
    refs[-1][...] = total.astype(jnp.bfloat16)


def row_sum(kept, got):
    shape = jax.ShapeDtypeStruct(kept.shape, jnp.bfloat16)
    return pl.pallas_call(row_sum_kernel, out_shape=shape, name="row_sum")(kept, *got)


def invert_factor(gram):
    n = gram.shape[0]
    pieces = n // SUB
    lane = lax.broadcasted_iota(jnp.int32, (SUB, n), 1)
    sub = lax.broadcasted_iota(jnp.int32, (SUB, n), 0)
    trace = jnp.zeros((SUB, n), jnp.float32)
    for v in range(pieces):
        trace = trace + jnp.where(lane == sub + v * SUB, gram[v * SUB : (v + 1) * SUB, :], 0.0)
    shift = (SHIFT / n) * jnp.sum(trace)
    a = [
        gram[v * SUB : (v + 1) * SUB, :] + jnp.where(lane == sub + v * SUB, shift, 0.0)
        for v in range(pieces)
    ]
    for b in range(pieces):
        cols = [
            {v: jnp.broadcast_to(a[v][:, b * SUB + c : b * SUB + c + 1], (SUB, n)) for v in range(b, pieces)}
            for c in range(SUB)
        ]
        for c in range(SUB):
            j = b * SUB + c
            pivot = jnp.broadcast_to(cols[c][b][c : c + 1, :], (SUB, n))
            inv = 1.0 / pivot
            row = jnp.broadcast_to(a[b][c : c + 1, :], (SUB, n))
            row = jnp.where(lane == j, 1.0, row)
            nexts = {
                c2: jnp.broadcast_to(cols[c2][b][c : c + 1, :], (SUB, n)) for c2 in range(c + 1, SUB)
            }
            for v in range(b, pieces):
                m = cols[c][v] * inv
                here = lane == j
                if v == b:
                    m = jnp.where(sub > c, m, 0.0)
                    here = here & (sub > c)
                a[v] = jnp.where(here, 0.0, a[v]) - m * row
                for c2 in range(c + 1, SUB):
                    cols[c2][v] = cols[c2][v] - m * nexts[c2]
    out = []
    for v in range(pieces):
        diag = lane == sub + v * SUB
        d = jnp.sum(jnp.where(diag, a[v], 0.0), axis=1, keepdims=True)
        low = jnp.where(lane < sub + v * SUB, a[v], jnp.where(diag, 1.0, 0.0))
        out.append(low * lax.rsqrt(d))
    return jnp.concatenate(out, axis=0)


def project_kernel(order_ref, *refs, panels, calls, own_at):
    low_refs = refs[: -(calls + 5)]
    tiles_hbm = refs[-(calls + 5) : -5]
    basis_ref, out_ref, low_all, held, sems = refs[-5:]
    per_call = tiles_hbm[0].shape[1]
    copies = [
        pltpu.make_async_copy(
            tiles_hbm[i], held.at[:, i * per_call : (i + 1) * per_call, :], sems.at[i]
        )
        for i in range(calls)
    ]
    for copy in copies:
        copy.start()
    count = order_ref[panels]
    out_ref[...] = jnp.zeros_like(out_ref)
    q = low_refs[0].shape[0]
    for i, ref in enumerate(low_refs):
        low_all[i * q : (i + 1) * q, :] = ref[...]
    low = low_all[...]
    low_t = low.T
    gram = jnp.dot(low_t, low, preferred_element_type=jnp.float32)
    inverse = invert_factor(gram)
    inv_t = [p.astype(jnp.bfloat16) for p in three(inverse.T)]
    for i, at in enumerate(own_at):
        own = low_refs[at][...]
        parts = [jnp.dot(own, p, preferred_element_type=jnp.float32) for p in inv_t]
        basis_ref[i * q : (i + 1) * q, :] = parts[0] + (parts[1] + parts[2])
    parts = [
        jnp.dot(p.astype(jnp.bfloat16), low_t, preferred_element_type=jnp.float32)
        for p in three(inverse)
    ]
    basis_t = (parts[0] + (parts[1] + parts[2])).astype(jnp.bfloat16)
    for copy in copies:
        copy.wait()

    def pair(j, carry):
        tile = jnp.concatenate([held[2 * j], held[2 * j + 1]], axis=1)
        cols = jnp.dot(basis_t, tile, preferred_element_type=jnp.float32).astype(jnp.bfloat16)
        at = pl.multiple_of(order_ref[2 * j] * WIDTH, WIDTH)
        out_ref[0, :, pl.ds(at, WIDTH)] = cols[:, :WIDTH]

        @pl.when(2 * j + 1 < count)
        def _():
            at = pl.multiple_of(order_ref[2 * j + 1] * WIDTH, WIDTH)
            out_ref[0, :, pl.ds(at, WIDTH)] = cols[:, WIDTH:]

        return carry

    lax.fori_loop(0, (count + 1) // 2, pair, 0)


def project_pass(order, lows, tiles, own_at, panels):
    rows = sum(t.shape[1] for t in tiles)
    held = tiles[0].shape[0]
    q, rank = lows[0].shape
    vmem = pl.BlockSpec(memory_space=pltpu.VMEM)
    return pl.pallas_call(
        functools.partial(project_kernel, panels=panels, calls=len(tiles), own_at=own_at),
        in_specs=[pl.BlockSpec(memory_space=pltpu.SMEM)]
        + [vmem] * len(lows)
        + [pl.BlockSpec(memory_space=pltpu.HBM)] * len(tiles),
        out_specs=[vmem, vmem],
        out_shape=[
            jax.ShapeDtypeStruct((q * len(own_at), rank), jnp.float32),
            jax.ShapeDtypeStruct((1, rank, panels * WIDTH), jnp.bfloat16),
        ],
        scratch_shapes=[
            pltpu.VMEM((rows, rank), jnp.bfloat16),
            pltpu.VMEM((held, rows, WIDTH), jnp.bfloat16),
            pltpu.SemaphoreType.DMA((len(tiles),)),
        ],
        compiler_params=pltpu.CompilerParams(vmem_limit_bytes=44 * 2**20),
        name="project_pass",
    )(order, *lows, *(in_hbm(x) for x in tiles))


def after(x, *deps):
    return lax.optimization_barrier((x, *deps))[0]


def swap(x, k, n):
    return lax.ppermute(x, "tile", [(i, i ^ k) for i in range(n)])


CHUNKS = 2


def local(row_points, source_points, sketch, admissible):
    n = lax.axis_size("tile")
    panels = admissible.shape[1]
    rows = row_points.shape[1] // lax.axis_size("row")
    own_rows = rows // n
    q = own_rows // CHUNKS
    odd, even = list(range(1, n, 2)), list(range(0, n, 2))
    slices = [(k, c * q, q) for c in range(CHUNKS) for k in odd + even]
    place = q % WIDTH == 0
    points = row_points
    if not place:
        me = lax.axis_index("tile")
        points = lax.dynamic_slice_in_dim(row_points, lax.axis_index("row") * rows, rows, 1)
        points = jnp.concatenate(
            [lax.dynamic_slice_in_dim(points, (me ^ k) * own_rows + first, q, 1) for k, first, _ in slices], 1
        )
    order, src_pick, omega_pick, row_mat = prep(
        admissible, points, source_points, sketch, rows, slices, place
    )

    call_rows = rows // CHUNKS // 2

    def sketch_part(at, *deps):
        return sketch_pass(
            after(order, *deps), src_pick, omega_pick, row_mat, at * call_rows, call_rows, panels
        )

    def sum_cores(got, own):
        kept, *sent = pair_sum(own, got, n // 2)
        return kept, [swap(x, k, n) for x, k in zip(sent, even[1:])]

    def spread(kept, got):
        low = row_sum(kept, got)
        held = [low] + [swap(low, k, n) for k in even[1:]]
        return [swap(x, 1, n) for x in held] + held

    lows, tiles, own_at, waiting = [], [], [], None
    last = ()
    for c in range(CHUNKS):
        theirs, kept = sketch_part(2 * c, *last)
        tiles.append(kept)
        got = swap(theirs, 1, n)
        if waiting is not None:
            lows += spread(after(waiting[0], theirs), waiting[1])
        own, kept = sketch_part(2 * c + 1, theirs, *lows[-n // 2 :][:1])
        tiles.append(kept)
        waiting = sum_cores(got, own)
        last = (own, waiting[0])
    lows += spread(*waiting)
    own_at = [c * n + n // 2 for c in range(CHUNKS)]
    return project_pass(order, lows, tiles, own_at, panels)


def solution(mesh):
    in_specs = (P(), P(None, "tile"), P("tile", None), P("row", "tile"))
    out_specs = (P(("row", "tile"), None), P("row", None, "tile"))
    return jax.shard_map(local, mesh=mesh, in_specs=in_specs, out_specs=out_specs, check_vma=False)
```

profile of v0, /device:TPU:15, one launch (start us, length us, event | category | flops | bytes accessed | tf_op | source)
XLA Modules:
  0.0 134.0 jit_solution(17399655235717454159)
XLA Ops:
  0.6 3.0 %prep.1 = (s32[40]{0:T(128)S(1)}, bf16[32,5120]{1,0:T(8,128)(2,1)S(1)}, bf16[5120,128]{1,0:T(8,128)(2,1)S(1)}, bf16[4096,32]{1,0:T(8,128)(2,1)S(1)}) custom-call(s32[1,32]{1,0:T(1,128)} %flags_hbm.1, f32[3,16384]{1,0:T(4,128)} %rows_hbm.1, f32[3,4096]{1,0:T(4,128)} %src_hbm.1, bf16[4096,128]{1,0:T(8,128)(2,1)} %omega_hbm.1), custom_call_target="tpu_custom_call" | custom-call | tf_op jit(solution)/shard_map/prep/pallas_call | solution.py:164
  3.6 17.1 %sketch_pass.4 = (f32[1024,128]{1,0:T(8,128)S(1)}, bf16[32,1024,128]{2,1,0:T(8,128)(2,1)}) custom-call(s32[40]{0:T(128)S(1)} %get-tuple-element.40.order_ref, bf16[32,5120]{1,0:T(8,128)(2,1)S(1)} %get-tuple-element.27.src_pick, bf16[5120,128]{1,0:T(8,128)(2,1)S(1)} %get-tuple-element.28.omega_pick, bf16[4096,32]{1,0:T(8,128)(2,1)S(1)} %get-tuple-element.29.row_mat), custom_call_target="tpu_custom_call" | custom-call | flops 8589934592 | bytes 8388608 | tf_op jit(solution)/shard_map/sketch_pass/pallas_call | solution.py:260
  20.7 0.1 collective-permute-start
  20.8 17.2 %sketch_pass.5 = (f32[1024,128]{1,0:T(8,128)S(1)}, bf16[32,1024,128]{2,1,0:T(8,128)(2,1)}) custom-call(s32[40]{0:T(128)S(1)} %get-tuple-element.40.order_ref, bf16[32,5120]{1,0:T(8,128)(2,1)S(1)} %get-tuple-element.27.src_pick, bf16[5120,128]{1,0:T(8,128)(2,1)S(1)} %get-tuple-element.28.omega_pick, bf16[4096,32]{1,0:T(8,128)(2,1)S(1)} %get-tuple-element.29.row_mat), custom_call_target="tpu_custom_call" | custom-call | flops 8589934592 | bytes 8388608 | tf_op jit(solution)/shard_map/sketch_pass/pallas_call | solution.py:260
  38.0 0.0 copy-start.1
  38.0 0.8 copy-done.1
  38.8 0.0 collective-permute-done.got_ref
  38.8 0.8 copy-done.6
  39.6 1.9 %pair_sum.2 = (f32[256,128]{1,0:T(8,128)}, bf16[256,128]{1,0:T(8,128)(2,1)}, bf16[256,128]{1,0:T(8,128)(2,1)}, bf16[256,128]{1,0:T(8,128)(2,1)}) custom-call(f32[1024,128]{1,0:T(8,128)} %copy-done.1, f32[1024,128]{1,0:T(8,128)} %copy-done.6), custom_call_target="tpu_custom_call" | custom-call | tf_op jit(solution)/shard_map/pair_sum/pallas_call | solution.py:297
  41.5 0.0 collective-permute-start.1
  41.5 0.0 collective-permute-start.2
  41.5 2.6 %collective-permute-start.3 = (bf16[256,128]{1,0:T(8,128)(2,1)}, bf16[256,128]{1,0:T(8,128)(2,1)S(1)}, u32[]{:S(2)}, u32[]{:S(2)}) collective-permute-start(bf16[256,128]{1,0:T(8,128)(2,1)} %get-tuple-element.39), channel_id=1, source_target_pairs={{0,6},{1,7},{2,4},{3,5},{4,2},{5,3},{6,0},{7,1},{8,14},{9,15},{10,... | collective-permute-start | bytes 196616 | tf_op jit(solution)/shard_map/ppermute | solution.py:438
  44.1 17.2 %sketch_pass.6 = (f32[1024,128]{1,0:T(8,128)S(1)}, bf16[32,1024,128]{2,1,0:T(8,128)(2,1)}) custom-call(s32[40]{0:T(128)S(1)} %get-tuple-element.40.order_ref, bf16[32,5120]{1,0:T(8,128)(2,1)S(1)} %get-tuple-element.27.src_pick, bf16[5120,128]{1,0:T(8,128)(2,1)S(1)} %get-tuple-element.28.omega_pick, bf16[4096,32]{1,0:T(8,128)(2,1)S(1)} %get-tuple-element.29.row_mat), custom_call_target="tpu_custom_call" | custom-call | flops 8589934592 | bytes 8388608 | tf_op jit(solution)/shard_map/sketch_pass/pallas_call | solution.py:260
  61.3 0.1 collective-permute-start.11
  61.4 0.0 collective-permute-done.1.refs_0_
  61.4 0.0 copy-start.10
  61.4 0.0 collective-permute-done.2.refs_1_
  61.4 0.0 collective-permute-done.3.refs_2_
  61.4 0.6 copy-done.10
  62.0 0.0 copy-done.11
  62.0 0.6 copy-done.12
  62.7 1.6 %row_sum.2.refs_4_ = bf16[256,128]{1,0:T(8,128)(2,1)} custom-call(f32[256,128]{1,0:T(8,128)} %get-tuple-element.36.kept_ref, bf16[256,128]{1,0:T(8,128)(2,1)} %copy-done.10, bf16[256,128]{1,0:T(8,128)(2,1)} %copy-done.11, bf16[256,128]{1,0:T(8,128)(2,1)} %copy-done.12), custom_call_target="tpu_custom_call" | custom-call | tf_op jit(solution)/shard_map/row_sum/pallas_call | solution.py:309
  64.3 0.0 collective-permute-start.9
  64.3 0.0 collective-permute-start.5
  64.3 1.0 copy-done.5
  65.3 17.1 %sketch_pass.7 = (f32[1024,128]{1,0:T(8,128)S(1)}, bf16[32,1024,128]{2,1,0:T(8,128)(2,1)}) custom-call(s32[40]{0:T(128)S(1)} %get-tuple-element.40.order_ref, bf16[32,5120]{1,0:T(8,128)(2,1)S(1)} %copy-done.5, bf16[5120,128]{1,0:T(8,128)(2,1)S(1)} %get-tuple-element.28.omega_pick, bf16[4096,32]{1,0:T(8,128)(2,1)S(1)} %get-tuple-element.29.row_mat), custom_call_target="tpu_custom_call" | custom-call | flops 8589934592 | bytes 8388608 | tf_op jit(solution)/shard_map/sketch_pass/pallas_call | solution.py:260
  82.4 0.0 copy-start
  82.4 0.8 copy-done
  83.2 0.0 collective-permute-done.11.got_ref
  83.2 1.9 %pair_sum.3 = (f32[256,128]{1,0:T(8,128)}, bf16[256,128]{1,0:T(8,128)(2,1)}, bf16[256,128]{1,0:T(8,128)(2,1)}, bf16[256,128]{1,0:T(8,128)(2,1)}) custom-call(f32[1024,128]{1,0:T(8,128)} %copy-done, f32[1024,128]{1,0:T(8,128)} %collective-permute-done.11.got_ref), custom_call_target="tpu_custom_call" | custom-call | tf_op jit(solution)/shard_map/pair_sum/pallas_call | solution.py:297
  85.1 0.0 collective-permute-start.12
  85.1 0.0 collective-permute-start.13
  85.1 2.6 %collective-permute-start.14 = (bf16[256,128]{1,0:T(8,128)(2,1)}, bf16[256,128]{1,0:T(8,128)(2,1)S(1)}, u32[]{:S(2)}, u32[]{:S(2)}) collective-permute-start(bf16[256,128]{1,0:T(8,128)(2,1)} %get-tuple-element.45), channel_id=1, source_target_pairs={{0,6},{1,7},{2,4},{3,5},{4,2},{5,3},{6,0},{7,1},{8,14},{9,15},{10,... | collective-permute-start | bytes 196616 | tf_op jit(solution)/shard_map/ppermute | solution.py:438
  87.8 0.0 collective-permute-done.9.refs_7_
  87.8 0.9 collective-permute-start.7
  88.7 0.0 collective-permute-done.5.refs_5_
  88.7 0.2 collective-permute-start.4
  88.9 0.2 collective-permute-done.12.refs_0_
  89.0 0.2 collective-permute-start.10
  89.2 0.2 collective-permute-done.13.refs_1_
  89.5 2.5 %collective-permute-start.6 = (bf16[256,128]{1,0:T(8,128)(2,1)S(1)}, bf16[256,128]{1,0:T(8,128)(2,1)S(1)}, u32[]{:S(2)}, u32[]{:S(2)}) collective-permute-start(bf16[256,128]{1,0:T(8,128)(2,1)S(1)} %collective-permute-done.5.refs_5_), channel_id=1, source_target_pairs={{0,1},{1,0},{2,3},{3,2},{4,5},{5,4},{6,7},{7,6},{8,9},{9,8},{10,11... | collective-permute-start | bytes 196616 | tf_op jit(solution)/shard_map/ppermute | solution.py:438
  91.9 3.8 %collective-permute-done.14.refs_2_ = bf16[256,128]{1,0:T(8,128)(2,1)S(1)} collective-permute-done((bf16[256,128]{1,0:T(8,128)(2,1)}, bf16[256,128]{1,0:T(8,128)(2,1)S(1)}, u32[]{:S(2)}, u32[]{:S(2)}) %collective-permute-start.14) | collective-permute-done | bytes 65568 | tf_op jit(solution)/shard_map/ppermute | solution.py:438
  95.7 0.6 copy-done.9
  96.3 1.6 %row_sum.3.refs_12_ = bf16[256,128]{1,0:T(8,128)(2,1)} custom-call(f32[256,128]{1,0:T(8,128)} %get-tuple-element.42.kept_ref, bf16[256,128]{1,0:T(8,128)(2,1)} %copy-done.7, bf16[256,128]{1,0:T(8,128)(2,1)} %copy-done.8, bf16[256,128]{1,0:T(8,128)(2,1)} %copy-done.9), custom_call_target="tpu_custom_call" | custom-call | tf_op jit(solution)/shard_map/row_sum/pallas_call | solution.py:309
  97.9 0.0 collective-permute-start.16
  97.9 0.0 collective-permute-done.7.refs_6_
  97.9 0.8 collective-permute-start.18
  98.8 0.0 collective-permute-done.4.refs_0_
  98.8 1.8 %collective-permute-start.20 = (bf16[256,128]{1,0:T(8,128)(2,1)}, bf16[256,128]{1,0:T(8,128)(2,1)S(1)}, u32[]{:S(2)}, u32[]{:S(2)}) collective-permute-start(bf16[256,128]{1,0:T(8,128)(2,1)} %row_sum.3.refs_12_), channel_id=1, source_target_pairs={{0,6},{1,7},{2,4},{3,5},{4,2},{5,3},{6,0},{7,1},{8,14},{9,15},{10,... | collective-permute-start | bytes 196616 | tf_op jit(solution)/shard_map/ppermute | solution.py:438
  100.6 0.0 collective-permute-done.10.refs_3_
  100.6 0.9 collective-permute-start.8
  101.5 0.0 collective-permute-done.6.refs_1_
  101.5 0.1 collective-permute-start.15
  101.6 0.2 collective-permute-done.16.refs_13_
  101.8 1.3 collective-permute-start.17
  103.1 0.0 collective-permute-done.18.refs_14_
  103.1 1.2 collective-permute-start.19
  104.4 2.8 %collective-permute-done.20.refs_15_ = bf16[256,128]{1,0:T(8,128)(2,1)S(1)} collective-permute-done((bf16[256,128]{1,0:T(8,128)(2,1)}, bf16[256,128]{1,0:T(8,128)(2,1)S(1)}, u32[]{:S(2)}, u32[]{:S(2)}) %collective-permute-start.20) | collective-permute-done | bytes 65568 | tf_op jit(solution)/shard_map/ppermute | solution.py:438
  107.2 0.7 collective-permute-start.21
  107.8 0.0 collective-permute-done.15.refs_8_
  107.8 0.0 collective-permute-done.17.refs_9_
  107.9 0.9 collective-permute-done.21.refs_11_
  108.7 0.8 copy-done.3
  109.6 24.4 %project_pass.1 = (f32[512,128]{1,0:T(8,128)}, bf16[1,128,4096]{2,1,0:T(8,128)(2,1)}) custom-call(s32[40]{0:T(128)S(1)} %get-tuple-element.40.order_ref, bf16[256,128]{1,0:T(8,128)(2,1)S(1)} %collective-permute-done.4.refs_0_, bf16[256,128]{1,0:T(8,128)(2,1)S(1)} %collective-permute-done.6.refs_1_, bf16[256,128]{1,0:T(8,128)(2,1)S(1)} %collective-permute-done.8.refs_2_, ...), custom_call_target="tpu_custom_call" | custom-call | tf_op jit(solution)/shard_map/project_pass/pallas_call | solution.py:413
  (16 shorter events, 0.0 us)
Async XLA Ops:
  3.6 40.5 %copy-start.4 = (bf16[32,5120]{1,0:T(8,128)(2,1)}, bf16[32,5120]{1,0:T(8,128)(2,1)S(1)}, u32[]{:S(2)}) copy-start(bf16[32,5120]{1,0:T(8,128)(2,1)S(1)} %get-tuple-element.27.src_pick) | copy-start | bytes 983044
  20.7 18.1 %collective-permute-start = (f32[1024,128]{1,0:T(8,128)S(1)}, f32[1024,128]{1,0:T(8,128)S(1)}, u32[]{:S(2)}, u32[]{:S(2)}) collective-permute-start(f32[1024,128]{1,0:T(8,128)S(1)} %get-tuple-element.30), channel_id=1, source_target_pairs={{0,1},{1,0},{2,3},{3,2},{4,5},{5,4},{6,7},{7,6},{8,9},{9,8},{10,11... | collective-permute-start | bytes 1572872 | tf_op jit(solution)/shard_map/ppermute | solution.py:438
  38.0 0.8 copy-start.1
  38.8 0.8 copy-start.6
  41.5 19.9 %collective-permute-start.1 = (bf16[256,128]{1,0:T(8,128)(2,1)}, bf16[256,128]{1,0:T(8,128)(2,1)S(1)}, u32[]{:S(2)}, u32[]{:S(2)}) collective-permute-start(bf16[256,128]{1,0:T(8,128)(2,1)} %get-tuple-element.37), channel_id=1, source_target_pairs={{0,2},{1,3},{2,0},{3,1},{4,6},{5,7},{6,4},{7,5},{8,10},{9,11},{10,... | collective-permute-start | bytes 196616 | tf_op jit(solution)/shard_map/ppermute | solution.py:438
  41.5 19.9 %collective-permute-start.2 = (bf16[256,128]{1,0:T(8,128)(2,1)}, bf16[256,128]{1,0:T(8,128)(2,1)S(1)}, u32[]{:S(2)}, u32[]{:S(2)}) collective-permute-start(bf16[256,128]{1,0:T(8,128)(2,1)} %get-tuple-element.38), channel_id=1, source_target_pairs={{0,4},{1,5},{2,6},{3,7},{4,0},{5,1},{6,2},{7,3},{8,12},{9,13},{10,... | collective-permute-start | bytes 196616 | tf_op jit(solution)/shard_map/ppermute | solution.py:438
  41.5 19.9 %collective-permute-start.3 = (bf16[256,128]{1,0:T(8,128)(2,1)}, bf16[256,128]{1,0:T(8,128)(2,1)S(1)}, u32[]{:S(2)}, u32[]{:S(2)}) collective-permute-start(bf16[256,128]{1,0:T(8,128)(2,1)} %get-tuple-element.39), channel_id=1, source_target_pairs={{0,6},{1,7},{2,4},{3,5},{4,2},{5,3},{6,0},{7,1},{8,14},{9,15},{10,... | collective-permute-start | bytes 196616 | tf_op jit(solution)/shard_map/ppermute | solution.py:438
  61.3 21.9 %collective-permute-start.11 = (f32[1024,128]{1,0:T(8,128)S(1)}, f32[1024,128]{1,0:T(8,128)}, u32[]{:S(2)}, u32[]{:S(2)}) collective-permute-start(f32[1024,128]{1,0:T(8,128)S(1)} %get-tuple-element.35), channel_id=1, source_target_pairs={{0,1},{1,0},{2,3},{3,2},{4,5},{5,4},{6,7},{7,6},{8,9},{9,8},{10,11... | collective-permute-start | bytes 1572872 | tf_op jit(solution)/shard_map/ppermute | solution.py:438
  61.4 0.6 copy-start.10
  61.4 0.6 copy-start.11
  62.0 0.6 copy-start.12
  64.3 23.5 %copy-start.2 = (bf16[256,128]{1,0:T(8,128)(2,1)S(1)}, bf16[256,128]{1,0:T(8,128)(2,1)}, u32[]{:S(2)}) copy-start(bf16[256,128]{1,0:T(8,128)(2,1)} %row_sum.2.refs_4_) | copy-start | bytes 196612
  64.3 23.5 %collective-permute-start.9 = (bf16[256,128]{1,0:T(8,128)(2,1)}, bf16[256,128]{1,0:T(8,128)(2,1)S(1)}, u32[]{:S(2)}, u32[]{:S(2)}) collective-permute-start(bf16[256,128]{1,0:T(8,128)(2,1)} %row_sum.2.refs_4_), channel_id=1, source_target_pairs={{0,6},{1,7},{2,4},{3,5},{4,2},{5,3},{6,0},{7,1},{8,14},{9,15},{10,... | collective-permute-start | bytes 196616 | tf_op jit(solution)/shard_map/ppermute | solution.py:438
  64.3 24.4 %collective-permute-start.5 = (bf16[256,128]{1,0:T(8,128)(2,1)}, bf16[256,128]{1,0:T(8,128)(2,1)S(1)}, u32[]{:S(2)}, u32[]{:S(2)}) collective-permute-start(bf16[256,128]{1,0:T(8,128)(2,1)} %row_sum.2.refs_4_), channel_id=1, source_target_pairs={{0,2},{1,3},{2,0},{3,1},{4,6},{5,7},{6,4},{7,5},{8,10},{9,11},{10,... | collective-permute-start | bytes 196616 | tf_op jit(solution)/shard_map/ppermute | solution.py:438
  64.3 1.0 copy-start.5
  82.4 0.8 copy-start
  85.1 3.9 %collective-permute-start.12 = (bf16[256,128]{1,0:T(8,128)(2,1)}, bf16[256,128]{1,0:T(8,128)(2,1)S(1)}, u32[]{:S(2)}, u32[]{:S(2)}) collective-permute-start(bf16[256,128]{1,0:T(8,128)(2,1)} %get-tuple-element.43), channel_id=1, source_target_pairs={{0,2},{1,3},{2,0},{3,1},{4,6},{5,7},{6,4},{7,5},{8,10},{9,11},{10,... | collective-permute-start | bytes 196616 | tf_op jit(solution)/shard_map/ppermute | solution.py:438
  85.1 4.3 %collective-permute-start.13 = (bf16[256,128]{1,0:T(8,128)(2,1)}, bf16[256,128]{1,0:T(8,128)(2,1)S(1)}, u32[]{:S(2)}, u32[]{:S(2)}) collective-permute-start(bf16[256,128]{1,0:T(8,128)(2,1)} %get-tuple-element.44), channel_id=1, source_target_pairs={{0,4},{1,5},{2,6},{3,7},{4,0},{5,1},{6,2},{7,3},{8,12},{9,13},{10,... | collective-permute-start | bytes 196616 | tf_op jit(solution)/shard_map/ppermute | solution.py:438
  85.1 10.6 %collective-permute-start.14 = (bf16[256,128]{1,0:T(8,128)(2,1)}, bf16[256,128]{1,0:T(8,128)(2,1)S(1)}, u32[]{:S(2)}, u32[]{:S(2)}) collective-permute-start(bf16[256,128]{1,0:T(8,128)(2,1)} %get-tuple-element.45), channel_id=1, source_target_pairs={{0,6},{1,7},{2,4},{3,5},{4,2},{5,3},{6,0},{7,1},{8,14},{9,15},{10,... | collective-permute-start | bytes 196616 | tf_op jit(solution)/shard_map/ppermute | solution.py:438
  87.8 10.2 %collective-permute-start.7 = (bf16[256,128]{1,0:T(8,128)(2,1)S(1)}, bf16[256,128]{1,0:T(8,128)(2,1)S(1)}, u32[]{:S(2)}, u32[]{:S(2)}) collective-permute-start(bf16[256,128]{1,0:T(8,128)(2,1)S(1)} %copy-done.2), channel_id=1, source_target_pairs={{0,4},{1,5},{2,6},{3,7},{4,0},{5,1},{6,2},{7,3},{8,12},{9,13},{10,... | collective-permute-start | bytes 196616 | tf_op jit(solution)/shard_map/ppermute | solution.py:438
  88.7 10.1 %collective-permute-start.4 = (bf16[256,128]{1,0:T(8,128)(2,1)S(1)}, bf16[256,128]{1,0:T(8,128)(2,1)S(1)}, u32[]{:S(2)}, u32[]{:S(2)}) collective-permute-start(bf16[256,128]{1,0:T(8,128)(2,1)S(1)} %copy-done.2), channel_id=1, source_target_pairs={{0,1},{1,0},{2,3},{3,2},{4,5},{5,4},{6,7},{7,6},{8,9},{9,8},{10,11... | collective-permute-start | bytes 196616 | tf_op jit(solution)/shard_map/ppermute | solution.py:438
  89.0 6.7 %copy-start.7 = (bf16[256,128]{1,0:T(8,128)(2,1)}, bf16[256,128]{1,0:T(8,128)(2,1)S(1)}, u32[]{:S(2)}) copy-start(bf16[256,128]{1,0:T(8,128)(2,1)S(1)} %collective-permute-done.12.refs_0_) | copy-start | bytes 196612
  89.0 11.6 %collective-permute-start.10 = (bf16[256,128]{1,0:T(8,128)(2,1)S(1)}, bf16[256,128]{1,0:T(8,128)(2,1)S(1)}, u32[]{:S(2)}, u32[]{:S(2)}) collective-permute-start(bf16[256,128]{1,0:T(8,128)(2,1)S(1)} %collective-permute-done.9.refs_7_), channel_id=1, source_target_pairs={{0,1},{1,0},{2,3},{3,2},{4,5},{5,4},{6,7},{7,6},{8,9},{9,8},{10,11... | collective-permute-start | bytes 196616 | tf_op jit(solution)/shard_map/ppermute | solution.py:438
  89.5 6.3 %copy-start.8 = (bf16[256,128]{1,0:T(8,128)(2,1)}, bf16[256,128]{1,0:T(8,128)(2,1)S(1)}, u32[]{:S(2)}) copy-start(bf16[256,128]{1,0:T(8,128)(2,1)S(1)} %collective-permute-done.13.refs_1_) | copy-start | bytes 196612
  89.5 12.1 %collective-permute-start.6 = (bf16[256,128]{1,0:T(8,128)(2,1)S(1)}, bf16[256,128]{1,0:T(8,128)(2,1)S(1)}, u32[]{:S(2)}, u32[]{:S(2)}) collective-permute-start(bf16[256,128]{1,0:T(8,128)(2,1)S(1)} %collective-permute-done.5.refs_5_), channel_id=1, source_target_pairs={{0,1},{1,0},{2,3},{3,2},{4,5},{5,4},{6,7},{7,6},{8,9},{9,8},{10,11... | collective-permute-start | bytes 196616 | tf_op jit(solution)/shard_map/ppermute | solution.py:438
  95.7 0.6 copy-start.9
  97.9 3.9 %collective-permute-start.16 = (bf16[256,128]{1,0:T(8,128)(2,1)}, bf16[256,128]{1,0:T(8,128)(2,1)S(1)}, u32[]{:S(2)}, u32[]{:S(2)}) collective-permute-start(bf16[256,128]{1,0:T(8,128)(2,1)} %row_sum.3.refs_12_), channel_id=1, source_target_pairs={{0,2},{1,3},{2,0},{3,1},{4,6},{5,7},{6,4},{7,5},{8,10},{9,11},{10,... | collective-permute-start | bytes 196616 | tf_op jit(solution)/shard_map/ppermute | solution.py:438
  97.9 5.2 %collective-permute-start.18 = (bf16[256,128]{1,0:T(8,128)(2,1)}, bf16[256,128]{1,0:T(8,128)(2,1)S(1)}, u32[]{:S(2)}, u32[]{:S(2)}) collective-permute-start(bf16[256,128]{1,0:T(8,128)(2,1)} %row_sum.3.refs_12_), channel_id=1, source_target_pairs={{0,4},{1,5},{2,6},{3,7},{4,0},{5,1},{6,2},{7,3},{8,12},{9,13},{10,... | collective-permute-start | bytes 196616 | tf_op jit(solution)/shard_map/ppermute | solution.py:438
  98.8 8.4 %collective-permute-start.20 = (bf16[256,128]{1,0:T(8,128)(2,1)}, bf16[256,128]{1,0:T(8,128)(2,1)S(1)}, u32[]{:S(2)}, u32[]{:S(2)}) collective-permute-start(bf16[256,128]{1,0:T(8,128)(2,1)} %row_sum.3.refs_12_), channel_id=1, source_target_pairs={{0,6},{1,7},{2,4},{3,5},{4,2},{5,3},{6,0},{7,1},{8,14},{9,15},{10,... | collective-permute-start | bytes 196616 | tf_op jit(solution)/shard_map/ppermute | solution.py:438
  100.6 7.2 %collective-permute-start.8 = (bf16[256,128]{1,0:T(8,128)(2,1)S(1)}, bf16[256,128]{1,0:T(8,128)(2,1)S(1)}, u32[]{:S(2)}, u32[]{:S(2)}) collective-permute-start(bf16[256,128]{1,0:T(8,128)(2,1)S(1)} %collective-permute-done.7.refs_6_), channel_id=1, source_target_pairs={{0,1},{1,0},{2,3},{3,2},{4,5},{5,4},{6,7},{7,6},{8,9},{9,8},{10,11... | collective-permute-start | bytes 196616 | tf_op jit(solution)/shard_map/ppermute | solution.py:438
  101.5 6.3 %collective-permute-start.15 = (bf16[256,128]{1,0:T(8,128)(2,1)}, bf16[256,128]{1,0:T(8,128)(2,1)S(1)}, u32[]{:S(2)}, u32[]{:S(2)}) collective-permute-start(bf16[256,128]{1,0:T(8,128)(2,1)} %row_sum.3.refs_12_), channel_id=1, source_target_pairs={{0,1},{1,0},{2,3},{3,2},{4,5},{5,4},{6,7},{7,6},{8,9},{9,8},{10,11... | collective-permute-start | bytes 196616 | tf_op jit(solution)/shard_map/ppermute | solution.py:438
  101.8 6.0 %collective-permute-start.17 = (bf16[256,128]{1,0:T(8,128)(2,1)S(1)}, bf16[256,128]{1,0:T(8,128)(2,1)S(1)}, u32[]{:S(2)}, u32[]{:S(2)}) collective-permute-start(bf16[256,128]{1,0:T(8,128)(2,1)S(1)} %collective-permute-done.16.refs_13_), channel_id=1, source_target_pairs={{0,1},{1,0},{2,3},{3,2},{4,5},{5,4},{6,7},{7,6},{8,9},{9,8},{10,11... | collective-permute-start | bytes 196616 | tf_op jit(solution)/shard_map/ppermute | solution.py:438
  103.1 4.7 %collective-permute-start.19 = (bf16[256,128]{1,0:T(8,128)(2,1)S(1)}, bf16[256,128]{1,0:T(8,128)(2,1)S(1)}, u32[]{:S(2)}, u32[]{:S(2)}) collective-permute-start(bf16[256,128]{1,0:T(8,128)(2,1)S(1)} %collective-permute-done.18.refs_14_), channel_id=1, source_target_pairs={{0,1},{1,0},{2,3},{3,2},{4,5},{5,4},{6,7},{7,6},{8,9},{9,8},{10,11... | collective-permute-start | bytes 196616 | tf_op jit(solution)/shard_map/ppermute | solution.py:438
  107.2 1.6 %collective-permute-start.21 = (bf16[256,128]{1,0:T(8,128)(2,1)S(1)}, bf16[256,128]{1,0:T(8,128)(2,1)S(1)}, u32[]{:S(2)}, u32[]{:S(2)}) collective-permute-start(bf16[256,128]{1,0:T(8,128)(2,1)S(1)} %collective-permute-done.20.refs_15_), channel_id=1, source_target_pairs={{0,1},{1,0},{2,3},{3,2},{4,5},{5,4},{6,7},{7,6},{8,9},{9,8},{10,11... | collective-permute-start | bytes 196616 | tf_op jit(solution)/shard_map/ppermute | solution.py:438
  108.7 0.8 copy-start.3
where the time goes:
time: 134 us
  Pallas kernels  103 us (77%)
  starting transfers between devices  16 us (12%)
  waiting for transfers between devices  8.13 us (6%)
  local copies, waits for them, and re-layouts  6.04 us (5%)
    pallas_call x4, Pallas kernels, sketch_pass(): pl.pallas_call(functools.partial(sketch_kernel, first=first, panels=panel...  68.6 us
    pallas_call x1, Pallas kernels, project_pass(): pl.pallas_call(functools.partial(project_kernel, panels=panels, calls=len...  24.4 us
    ppermute x22, starting transfers between devices, swap(): return lax.ppermute(x, 'tile', [(i, i ^ k) for i in range(n)])  16 us
    ppermute x22, waiting for transfers between devices, swap(): return lax.ppermute(x, 'tile', [(i, i ^ k) for i in range(n)])  8.13 us
    unnamed x26, local copies, waits for them, and re-layouts  6.04 us
    pallas_call x2, Pallas kernels, pair_sum(): pl.pallas_call(pair_sum_kernel, out_shape=shapes, name='pair_sum')(own, got)  3.82 us
    pallas_call x2, Pallas kernels, row_sum(): pl.pallas_call(row_sum_kernel, out_shape=shape, name='row_sum')(kept, *got)  3.23 us
    pallas_call x1, Pallas kernels, prep(): pl.pallas_call(functools.partial(prep_kernel, slices=slices, place=place)...  2.96 us
  transfers between devices with their start and end apart: 22, of which 6 were waited for; matrix products, arithmetic and copies ran while one was open for 0% of the time, Pallas kernels for 42%

commit v1 on v0

--- a/solution.py
+++ b/solution.py
@@ -13,8 +13,9 @@
 SHIFT = 0.0001
 
 TURNS = WAVENUM / (2.0 * math.pi)
-DECAY = -DAMPING / TURNS / math.log(2.0)
-AMP = TURNS / (4.0 * math.pi)
+E3 = -5.419141508131567e-07
+E2, E1, E0 = 0.00012955130357743643 / E3, -0.016325949681618327 / E3, 0.9999205420269909 / E3
+AMP = TURNS / (4.0 * math.pi) * E3**4
 S0, S1, S2 = 6.28127979 * AMP, -41.0952178 * AMP, 73.5851113 * AMP
 
 WIDTH = 128
@@ -64,8 +65,9 @@
     g = 0.25 - jnp.abs(f)
     v = g * g
     wave = ((S2 * v + S1) * v + S0) * g
-    amp = jnp.exp2(DECAY * t) * inv
-    return (wave * amp).astype(jnp.bfloat16)
+    fade = ((t + E2) * t + E1) * t + E0
+    fade = fade * fade
+    return (wave * inv * (fade * fade)).astype(jnp.bfloat16)
 
 
 def order_panels(flags_ref, order_ref, panels):
@@ -279,11 +281,26 @@
     )(order, src_pick, omega_pick, row_mat)
 
 
+def in_vmem(kernel, out_shape, name):
+    def call(*args):
+        vmem = pl.BlockSpec(memory_space=pltpu.VMEM)
+        return pl.pallas_call(
+            kernel,
+            in_specs=[vmem] * len(args),
+            out_specs=jax.tree.map(lambda _: vmem, out_shape),
+            out_shape=out_shape,
+            compiler_params=pltpu.CompilerParams(vmem_limit_bytes=8 * 2**20),
+            name=name,
+        )(*args)
+
+    return call
+
+
 def pair_sum_kernel(own_ref, got_ref, kept_ref, *sent_refs):
     q = kept_ref.shape[0]
     for k in range(1 + len(sent_refs)):
         part = slice(k * q, (k + 1) * q)
-        value = own_ref[part, :] + got_ref[part, :].astype(jnp.float32)
+        value = own_ref[part, :] + got_ref[part, :]
         if k == 0:
             kept_ref[...] = value
         else:
@@ -294,19 +311,20 @@
     q, rank = own.shape[0] // slots, own.shape[1]
     shapes = [jax.ShapeDtypeStruct((q, rank), jnp.float32)]
     shapes += [jax.ShapeDtypeStruct((q, rank), jnp.bfloat16)] * (slots - 1)
-    return pl.pallas_call(pair_sum_kernel, out_shape=shapes, name="pair_sum")(own, got)
+    return in_vmem(pair_sum_kernel, shapes, "pair_sum")(own, got)
 
 
 def row_sum_kernel(kept_ref, *refs):
     total = kept_ref[...]
     for ref in refs[:-1]:
         total = total + ref[...].astype(jnp.float32)
-    refs[-1][...] = total.astype(jnp.bfloat16)
-
-
-def row_sum(kept, got):
-    shape = jax.ShapeDtypeStruct(kept.shape, jnp.bfloat16)
-    return pl.pallas_call(row_sum_kernel, out_shape=shape, name="row_sum")(kept, *got)
+    low = head(total)
+    refs[-1][...] = (low if refs[-1].shape == low.shape else low.T).astype(jnp.bfloat16)
+
+
+def row_sum(kept, got, flip):
+    shape = kept.shape[::-1] if flip else kept.shape
+    return in_vmem(row_sum_kernel, jax.ShapeDtypeStruct(shape, jnp.bfloat16), "row_sum")(kept, *got)
 
 
 def invert_factor(gram):
@@ -354,7 +372,7 @@
     return jnp.concatenate(out, axis=0)
 
 
-def project_kernel(order_ref, *refs, panels, calls, own_at):
+def project_kernel(order_ref, *refs, panels, calls, own_at, flip):
     low_refs = refs[: -(calls + 5)]
     tiles_hbm = refs[-(calls + 5) : -5]
     basis_ref, out_ref, low_all, held, sems = refs[-5:]
@@ -368,50 +386,48 @@
     for copy in copies:
         copy.start()
     count = order_ref[panels]
+    q = low_refs[0].shape[1 if flip else 0]
+    for i, ref in enumerate(low_refs):
+        if flip:
+            low_all[:, i * q : (i + 1) * q] = ref[...]
+        else:
+            low_all[i * q : (i + 1) * q, :] = ref[...]
+    low_t = low_all[...] if flip else low_all[...].T
+    gram = lax.dot_general(low_t, low_t, (((1,), (1,)), ((), ())), preferred_element_type=jnp.float32)
+    inverse = [p.astype(jnp.bfloat16) for p in three(invert_factor(gram))]
     out_ref[...] = jnp.zeros_like(out_ref)
-    q = low_refs[0].shape[0]
-    for i, ref in enumerate(low_refs):
-        low_all[i * q : (i + 1) * q, :] = ref[...]
-    low = low_all[...]
-    low_t = low.T
-    gram = jnp.dot(low_t, low, preferred_element_type=jnp.float32)
-    inverse = invert_factor(gram)
-    inv_t = [p.astype(jnp.bfloat16) for p in three(inverse.T)]
+    parts = [jnp.dot(p, low_t, preferred_element_type=jnp.float32) for p in inverse]
+    basis = parts[0] + (parts[1] + parts[2])
+    basis_t = basis.astype(jnp.bfloat16)
     for i, at in enumerate(own_at):
-        own = low_refs[at][...]
-        parts = [jnp.dot(own, p, preferred_element_type=jnp.float32) for p in inv_t]
-        basis_ref[i * q : (i + 1) * q, :] = parts[0] + (parts[1] + parts[2])
-    parts = [
-        jnp.dot(p.astype(jnp.bfloat16), low_t, preferred_element_type=jnp.float32)
-        for p in three(inverse)
-    ]
-    basis_t = (parts[0] + (parts[1] + parts[2])).astype(jnp.bfloat16)
+        basis_ref[i * q : (i + 1) * q, :] = basis[:, at * q : (at + 1) * q].T
     for copy in copies:
         copy.wait()
 
-    def pair(j, carry):
-        tile = jnp.concatenate([held[2 * j], held[2 * j + 1]], axis=1)
+    def group(j, carry):
+        tile = jnp.concatenate([held[GROUP * j + k] for k in range(GROUP)], axis=1)
         cols = jnp.dot(basis_t, tile, preferred_element_type=jnp.float32).astype(jnp.bfloat16)
-        at = pl.multiple_of(order_ref[2 * j] * WIDTH, WIDTH)
-        out_ref[0, :, pl.ds(at, WIDTH)] = cols[:, :WIDTH]
-
-        @pl.when(2 * j + 1 < count)
-        def _():
-            at = pl.multiple_of(order_ref[2 * j + 1] * WIDTH, WIDTH)
-            out_ref[0, :, pl.ds(at, WIDTH)] = cols[:, WIDTH:]
+        for k in range(GROUP):
+
+            @pl.when(GROUP * j + k < count)
+            def _():
+                at = pl.multiple_of(order_ref[GROUP * j + k] * WIDTH, WIDTH)
+                out_ref[0, :, pl.ds(at, WIDTH)] = cols[:, k * WIDTH : (k + 1) * WIDTH]
 
         return carry
 
-    lax.fori_loop(0, (count + 1) // 2, pair, 0)
-
-
-def project_pass(order, lows, tiles, own_at, panels):
+    lax.fori_loop(0, (count + GROUP - 1) // GROUP, group, 0)
+
+
+def project_pass(order, lows, tiles, own_at, panels, rank, flip):
     rows = sum(t.shape[1] for t in tiles)
     held = tiles[0].shape[0]
-    q, rank = lows[0].shape
+    q = lows[0].shape[1 if flip else 0]
     vmem = pl.BlockSpec(memory_space=pltpu.VMEM)
     return pl.pallas_call(
-        functools.partial(project_kernel, panels=panels, calls=len(tiles), own_at=own_at),
+        functools.partial(
+            project_kernel, panels=panels, calls=len(tiles), own_at=own_at, flip=flip
+        ),
         in_specs=[pl.BlockSpec(memory_space=pltpu.SMEM)]
         + [vmem] * len(lows)
         + [pl.BlockSpec(memory_space=pltpu.HBM)] * len(tiles),
@@ -421,11 +437,11 @@
             jax.ShapeDtypeStruct((1, rank, panels * WIDTH), jnp.bfloat16),
         ],
         scratch_shapes=[
-            pltpu.VMEM((rows, rank), jnp.bfloat16),
+            pltpu.VMEM((rank, rows) if flip else (rows, rank), jnp.bfloat16),
             pltpu.VMEM((held, rows, WIDTH), jnp.bfloat16),
             pltpu.SemaphoreType.DMA((len(tiles),)),
         ],
-        compiler_params=pltpu.CompilerParams(vmem_limit_bytes=44 * 2**20),
+        compiler_params=pltpu.CompilerParams(vmem_limit_bytes=48 * 2**20),
         name="project_pass",
     )(order, *lows, *(in_hbm(x) for x in tiles))
 
@@ -449,7 +465,7 @@
     q = own_rows // CHUNKS
     odd, even = list(range(1, n, 2)), list(range(0, n, 2))
     slices = [(k, c * q, q) for c in range(CHUNKS) for k in odd + even]
-    place = q % WIDTH == 0
+    place = flip = q % WIDTH == 0
     points = row_points
     if not place:
         me = lax.axis_index("tile")
@@ -473,7 +489,7 @@
         return kept, [swap(x, k, n) for x, k in zip(sent, even[1:])]
 
     def spread(kept, got):
-        low = row_sum(kept, got)
+        low = row_sum(kept, got, flip)
         held = [low] + [swap(low, k, n) for k in even[1:]]
         return [swap(x, 1, n) for x in held] + held
 
@@ -491,7 +507,7 @@
         last = (own, waiting[0])
     lows += spread(*waiting)
     own_at = [c * n + n // 2 for c in range(CHUNKS)]
-    return project_pass(order, lows, tiles, own_at, panels)
+    return project_pass(order, lows, tiles, own_at, panels, sketch.shape[1], flip)
 
 
 def solution(mesh):

time: 134 us -> 134 us (level)
  the two profiles are of different devices: /device:TPU:15 before, /device:TPU:4 now
where the time goes in v1:
time: 134 us; the launch traced here: 135 us
  Pallas kernels  107 us (80%)
  starting transfers between devices  17.5 us (13%)
  waiting for transfers between devices  9.92 us (7%)
    pallas_call x4, Pallas kernels, sketch_pass(): pl.pallas_call(functools.partial(sketch_kernel, first=first, panels=panel...  79.4 us
    pallas_call x1, Pallas kernels, project_pass(): pl.pallas_call(functools.partial(project_kernel, panels=panels, calls=len...  24.3 us
    ppermute x22, starting transfers between devices, swap(): return lax.ppermute(x, 'tile', [(i, i ^ k) for i in range(n)])  17.5 us
    ppermute x22, waiting for transfers between devices, swap(): return lax.ppermute(x, 'tile', [(i, i ^ k) for i in range(n)])  9.92 us
    pallas_call x1, Pallas kernels, prep(): pl.pallas_call(functools.partial(prep_kernel, slices=slices, place=place)...  2.94 us
  transfers between devices with their start and end apart: 22, of which 6 were waited for; matrix products, arithmetic and copies ran while one was open for 0% of the time, Pallas kernels for 44%

profile of v1, /device:TPU:4, one launch (start us, length us, event | category | flops | bytes accessed | tf_op | source)
XLA Modules:
  0.0 135.4 jit_solution(4958960012352255087)
XLA Ops:
  0.6 2.9 %prep.1 = (s32[40]{0:T(128)S(1)}, bf16[32,5120]{1,0:T(8,128)(2,1)S(1)}, bf16[5120,128]{1,0:T(8,128)(2,1)S(1)}, bf16[4096,32]{1,0:T(8,128)(2,1)S(1)}) custom-call(s32[1,32]{1,0:T(1,128)} %flags_hbm.1, f32[3,16384]{1,0:T(4,128)} %rows_hbm.1, f32[3,4096]{1,0:T(4,128)} %src_hbm.1, bf16[4096,128]{1,0:T(8,128)(2,1)} %omega_hbm.1), custom_call_target="tpu_custom_call" | custom-call | tf_op jit(solution)/shard_map/prep/pallas_call | solution.py:166
  3.6 19.8 %sketch_pass.4 = (f32[1024,128]{1,0:T(8,128)S(1)}, bf16[32,1024,128]{2,1,0:T(8,128)(2,1)}) custom-call(s32[40]{0:T(128)S(1)} %get-tuple-element.40.order_ref, bf16[32,5120]{1,0:T(8,128)(2,1)S(1)} %get-tuple-element.27.src_pick, bf16[5120,128]{1,0:T(8,128)(2,1)S(1)} %get-tuple-element.28.omega_pick, bf16[4096,32]{1,0:T(8,128)(2,1)S(1)} %get-tuple-element.29.row_mat), custom_call_target="tpu_custom_call" | custom-call | flops 8589934592 | bytes 8388608 | tf_op jit(solution)/shard_map/sketch_pass/pallas_call | solution.py:262
  23.4 0.1 collective-permute-start
  23.4 19.8 %sketch_pass.5 = (f32[1024,128]{1,0:T(8,128)S(1)}, bf16[32,1024,128]{2,1,0:T(8,128)(2,1)}) custom-call(s32[40]{0:T(128)S(1)} %get-tuple-element.40.order_ref, bf16[32,5120]{1,0:T(8,128)(2,1)S(1)} %get-tuple-element.27.src_pick, bf16[5120,128]{1,0:T(8,128)(2,1)S(1)} %get-tuple-element.28.omega_pick, bf16[4096,32]{1,0:T(8,128)(2,1)S(1)} %get-tuple-element.29.row_mat), custom_call_target="tpu_custom_call" | custom-call | flops 8589934592 | bytes 8388608 | tf_op jit(solution)/shard_map/sketch_pass/pallas_call | solution.py:262
  43.3 0.0 collective-permute-done.got_ref
  43.3 0.1 pair_sum.2
  43.3 0.1 collective-permute-start.1
  43.4 0.1 collective-permute-start.2
  43.5 4.3 %collective-permute-start.3 = (bf16[256,128]{1,0:T(8,128)(2,1)S(1)}, bf16[256,128]{1,0:T(8,128)(2,1)S(1)}, u32[]{:S(2)}, u32[]{:S(2)}) collective-permute-start(bf16[256,128]{1,0:T(8,128)(2,1)S(1)} %get-tuple-element.39), channel_id=1, source_target_pairs={{0,6},{1,7},{2,4},{3,5},{4,2},{5,3},{6,0},{7,1},{8,14},{9,15},{10,... | collective-permute-start | bytes 196616 | tf_op jit(solution)/shard_map/ppermute | solution.py:454
  47.8 19.8 %sketch_pass.6 = (f32[1024,128]{1,0:T(8,128)S(1)}, bf16[32,1024,128]{2,1,0:T(8,128)(2,1)}) custom-call(s32[40]{0:T(128)S(1)} %get-tuple-element.40.order_ref, bf16[32,5120]{1,0:T(8,128)(2,1)S(1)} %get-tuple-element.27.src_pick, bf16[5120,128]{1,0:T(8,128)(2,1)S(1)} %get-tuple-element.28.omega_pick, bf16[4096,32]{1,0:T(8,128)(2,1)S(1)} %get-tuple-element.29.row_mat), custom_call_target="tpu_custom_call" | custom-call | flops 8589934592 | bytes 8388608 | tf_op jit(solution)/shard_map/sketch_pass/pallas_call | solution.py:262
  67.6 0.1 collective-permute-start.11
  67.7 0.0 collective-permute-done.1.refs_0_
  67.7 0.0 collective-permute-done.2.refs_1_
  67.7 0.0 collective-permute-done.3.refs_2_
  67.7 0.1 row_sum.2.refs_4_
  67.8 0.1 collective-permute-start.9
  67.9 1.2 collective-permute-start.5
  69.1 20.0 %sketch_pass.7 = (f32[1024,128]{1,0:T(8,128)S(1)}, bf16[32,1024,128]{2,1,0:T(8,128)(2,1)}) custom-call(s32[40]{0:T(128)S(1)} %get-tuple-element.40.order_ref, bf16[32,5120]{1,0:T(8,128)(2,1)S(1)} %get-tuple-element.27.src_pick, bf16[5120,128]{1,0:T(8,128)(2,1)S(1)} %get-tuple-element.28.omega_pick, bf16[4096,32]{1,0:T(8,128)(2,1)S(1)} %get-tuple-element.29.row_mat), custom_call_target="tpu_custom_call" | custom-call | flops 8589934592 | bytes 8388608 | tf_op jit(solution)/shard_map/sketch_pass/pallas_call | solution.py:262
  89.1 0.0 collective-permute-done.11.got_ref
  89.1 0.1 pair_sum.3
  89.2 0.1 collective-permute-start.12
  89.3 0.1 collective-permute-start.13
  89.4 4.3 %collective-permute-start.14 = (bf16[256,128]{1,0:T(8,128)(2,1)S(1)}, bf16[256,128]{1,0:T(8,128)(2,1)S(1)}, u32[]{:S(2)}, u32[]{:S(2)}) collective-permute-start(bf16[256,128]{1,0:T(8,128)(2,1)S(1)} %get-tuple-element.45), channel_id=1, source_target_pairs={{0,6},{1,7},{2,4},{3,5},{4,2},{5,3},{6,0},{7,1},{8,14},{9,15},{10,... | collective-permute-start | bytes 196616 | tf_op jit(solution)/shard_map/ppermute | solution.py:454
  93.7 0.0 collective-permute-done.9.refs_7_
  93.7 0.0 collective-permute-start.7
  93.7 0.0 collective-permute-done.5.refs_5_
  93.7 1.0 collective-permute-start.4
  94.7 0.0 collective-permute-done.12.refs_0_
  94.7 0.1 collective-permute-start.10
  94.8 0.2 collective-permute-done.13.refs_1_
  94.9 0.3 collective-permute-start.6
  95.2 2.7 %collective-permute-done.14.refs_2_ = bf16[256,128]{1,0:T(8,128)(2,1)S(1)} collective-permute-done((bf16[256,128]{1,0:T(8,128)(2,1)S(1)}, bf16[256,128]{1,0:T(8,128)(2,1)S(1)}, u32[]{:S(2)}, u32[]{:S(2)}) %collective-permute-start.14) | collective-permute-done | bytes 65568 | tf_op jit(solution)/shard_map/ppermute | solution.py:454
  97.9 0.1 row_sum.3.refs_12_
  98.0 2.9 %collective-permute-start.16 = (bf16[128,256]{1,0:T(8,128)(2,1)S(1)}, bf16[128,256]{1,0:T(8,128)(2,1)S(1)}, u32[]{:S(2)}, u32[]{:S(2)}) collective-permute-start(bf16[128,256]{1,0:T(8,128)(2,1)S(1)} %row_sum.3.refs_12_), channel_id=1, source_target_pairs={{0,2},{1,3},{2,0},{3,1},{4,6},{5,7},{6,4},{7,5},{8,10},{9,11},{10,... | collective-permute-start | bytes 196616 | tf_op jit(solution)/shard_map/ppermute | solution.py:454
  101.0 0.7 collective-permute-done.7.refs_6_
  101.6 1.0 collective-permute-start.18
  102.7 0.0 collective-permute-done.4.refs_0_
  102.7 0.7 collective-permute-start.20
  103.4 0.0 collective-permute-done.10.refs_3_
  103.4 0.0 collective-permute-start.8
  103.4 0.0 collective-permute-done.6.refs_1_
  103.4 0.5 collective-permute-start.15
  104.0 0.0 collective-permute-done.16.refs_13_
  104.0 0.1 collective-permute-start.17
  104.0 5.5 %collective-permute-done.18.refs_14_ = bf16[128,256]{1,0:T(8,128)(2,1)S(1)} collective-permute-done((bf16[128,256]{1,0:T(8,128)(2,1)S(1)}, bf16[128,256]{1,0:T(8,128)(2,1)S(1)}, u32[]{:S(2)}, u32[]{:S(2)}) %collective-permute-start.18) | collective-permute-done | bytes 65568 | tf_op jit(solution)/shard_map/ppermute | solution.py:454
  109.5 0.0 collective-permute-start.19
  109.5 0.0 collective-permute-done.20.refs_15_
  109.5 0.5 collective-permute-start.21
  110.0 0.0 collective-permute-done.8.refs_2_
  110.0 0.0 collective-permute-done.15.refs_8_
  110.0 0.0 collective-permute-done.17.refs_9_
  110.0 0.7 collective-permute-done.19.refs_10_
  110.8 0.2 collective-permute-done.21.refs_11_
  110.9 24.3 %project_pass.1 = (f32[512,128]{1,0:T(8,128)}, bf16[1,128,4096]{2,1,0:T(8,128)(2,1)}) custom-call(s32[40]{0:T(128)S(1)} %get-tuple-element.40.order_ref, bf16[128,256]{1,0:T(8,128)(2,1)S(1)} %collective-permute-done.4.refs_0_, bf16[128,256]{1,0:T(8,128)(2,1)S(1)} %collective-permute-done.6.refs_1_, bf16[128,256]{1,0:T(8,128)(2,1)S(1)} %collective-permute-done.8.refs_2_, ...), custom_call_target="tpu_custom_call" | custom-call | tf_op jit(solution)/shard_map/project_pass/pallas_call | solution.py:427
Async XLA Ops:
  23.4 19.9 %collective-permute-start = (f32[1024,128]{1,0:T(8,128)S(1)}, f32[1024,128]{1,0:T(8,128)S(1)}, u32[]{:S(2)}, u32[]{:S(2)}) collective-permute-start(f32[1024,128]{1,0:T(8,128)S(1)} %get-tuple-element.30), channel_id=1, source_target_pairs={{0,1},{1,0},{2,3},{3,2},{4,5},{5,4},{6,7},{7,6},{8,9},{9,8},{10,11... | collective-permute-start | bytes 1572872 | tf_op jit(solution)/shard_map/ppermute | solution.py:454
  43.3 24.3 %collective-permute-start.1 = (bf16[256,128]{1,0:T(8,128)(2,1)S(1)}, bf16[256,128]{1,0:T(8,128)(2,1)S(1)}, u32[]{:S(2)}, u32[]{:S(2)}) collective-permute-start(bf16[256,128]{1,0:T(8,128)(2,1)S(1)} %get-tuple-element.37), channel_id=1, source_target_pairs={{0,2},{1,3},{2,0},{3,1},{4,6},{5,7},{6,4},{7,5},{8,10},{9,11},{10,... | collective-permute-start | bytes 196616 | tf_op jit(solution)/shard_map/ppermute | solution.py:454
  43.4 24.2 %collective-permute-start.2 = (bf16[256,128]{1,0:T(8,128)(2,1)S(1)}, bf16[256,128]{1,0:T(8,128)(2,1)S(1)}, u32[]{:S(2)}, u32[]{:S(2)}) collective-permute-start(bf16[256,128]{1,0:T(8,128)(2,1)S(1)} %get-tuple-element.38), channel_id=1, source_target_pairs={{0,4},{1,5},{2,6},{3,7},{4,0},{5,1},{6,2},{7,3},{8,12},{9,13},{10,... | collective-permute-start | bytes 196616 | tf_op jit(solution)/shard_map/ppermute | solution.py:454
  43.5 24.2 %collective-permute-start.3 = (bf16[256,128]{1,0:T(8,128)(2,1)S(1)}, bf16[256,128]{1,0:T(8,128)(2,1)S(1)}, u32[]{:S(2)}, u32[]{:S(2)}) collective-permute-start(bf16[256,128]{1,0:T(8,128)(2,1)S(1)} %get-tuple-element.39), channel_id=1, source_target_pairs={{0,6},{1,7},{2,4},{3,5},{4,2},{5,3},{6,0},{7,1},{8,14},{9,15},{10,... | collective-permute-start | bytes 196616 | tf_op jit(solution)/shard_map/ppermute | solution.py:454
  67.6 21.6 %collective-permute-start.11 = (f32[1024,128]{1,0:T(8,128)S(1)}, f32[1024,128]{1,0:T(8,128)S(1)}, u32[]{:S(2)}, u32[]{:S(2)}) collective-permute-start(f32[1024,128]{1,0:T(8,128)S(1)} %get-tuple-element.35), channel_id=1, source_target_pairs={{0,1},{1,0},{2,3},{3,2},{4,5},{5,4},{6,7},{7,6},{8,9},{9,8},{10,11... | collective-permute-start | bytes 1572872 | tf_op jit(solution)/shard_map/ppermute | solution.py:454
  67.8 25.9 %collective-permute-start.9 = (bf16[128,256]{1,0:T(8,128)(2,1)S(1)}, bf16[128,256]{1,0:T(8,128)(2,1)S(1)}, u32[]{:S(2)}, u32[]{:S(2)}) collective-permute-start(bf16[128,256]{1,0:T(8,128)(2,1)S(1)} %row_sum.2.refs_4_), channel_id=1, source_target_pairs={{0,6},{1,7},{2,4},{3,5},{4,2},{5,3},{6,0},{7,1},{8,14},{9,15},{10,... | collective-permute-start | bytes 196616 | tf_op jit(solution)/shard_map/ppermute | solution.py:454
  67.9 25.8 %collective-permute-start.5 = (bf16[128,256]{1,0:T(8,128)(2,1)S(1)}, bf16[128,256]{1,0:T(8,128)(2,1)S(1)}, u32[]{:S(2)}, u32[]{:S(2)}) collective-permute-start(bf16[128,256]{1,0:T(8,128)(2,1)S(1)} %row_sum.2.refs_4_), channel_id=1, source_target_pairs={{0,2},{1,3},{2,0},{3,1},{4,6},{5,7},{6,4},{7,5},{8,10},{9,11},{10,... | collective-permute-start | bytes 196616 | tf_op jit(solution)/shard_map/ppermute | solution.py:454
  89.2 5.5 %collective-permute-start.12 = (bf16[256,128]{1,0:T(8,128)(2,1)S(1)}, bf16[256,128]{1,0:T(8,128)(2,1)S(1)}, u32[]{:S(2)}, u32[]{:S(2)}) collective-permute-start(bf16[256,128]{1,0:T(8,128)(2,1)S(1)} %get-tuple-element.43), channel_id=1, source_target_pairs={{0,2},{1,3},{2,0},{3,1},{4,6},{5,7},{6,4},{7,5},{8,10},{9,11},{10,... | collective-permute-start | bytes 196616 | tf_op jit(solution)/shard_map/ppermute | solution.py:454
  89.3 5.7 %collective-permute-start.13 = (bf16[256,128]{1,0:T(8,128)(2,1)S(1)}, bf16[256,128]{1,0:T(8,128)(2,1)S(1)}, u32[]{:S(2)}, u32[]{:S(2)}) collective-permute-start(bf16[256,128]{1,0:T(8,128)(2,1)S(1)} %get-tuple-element.44), channel_id=1, source_target_pairs={{0,4},{1,5},{2,6},{3,7},{4,0},{5,1},{6,2},{7,3},{8,12},{9,13},{10,... | collective-permute-start | bytes 196616 | tf_op jit(solution)/shard_map/ppermute | solution.py:454
  89.4 8.6 %collective-permute-start.14 = (bf16[256,128]{1,0:T(8,128)(2,1)S(1)}, bf16[256,128]{1,0:T(8,128)(2,1)S(1)}, u32[]{:S(2)}, u32[]{:S(2)}) collective-permute-start(bf16[256,128]{1,0:T(8,128)(2,1)S(1)} %get-tuple-element.45), channel_id=1, source_target_pairs={{0,6},{1,7},{2,4},{3,5},{4,2},{5,3},{6,0},{7,1},{8,14},{9,15},{10,... | collective-permute-start | bytes 196616 | tf_op jit(solution)/shard_map/ppermute | solution.py:454
  93.7 8.0 %collective-permute-start.7 = (bf16[128,256]{1,0:T(8,128)(2,1)S(1)}, bf16[128,256]{1,0:T(8,128)(2,1)S(1)}, u32[]{:S(2)}, u32[]{:S(2)}) collective-permute-start(bf16[128,256]{1,0:T(8,128)(2,1)S(1)} %row_sum.2.refs_4_), channel_id=1, source_target_pairs={{0,4},{1,5},{2,6},{3,7},{4,0},{5,1},{6,2},{7,3},{8,12},{9,13},{10,... | collective-permute-start | bytes 196616 | tf_op jit(solution)/shard_map/ppermute | solution.py:454
  93.7 9.0 %collective-permute-start.4 = (bf16[128,256]{1,0:T(8,128)(2,1)S(1)}, bf16[128,256]{1,0:T(8,128)(2,1)S(1)}, u32[]{:S(2)}, u32[]{:S(2)}) collective-permute-start(bf16[128,256]{1,0:T(8,128)(2,1)S(1)} %row_sum.2.refs_4_), channel_id=1, source_target_pairs={{0,1},{1,0},{2,3},{3,2},{4,5},{5,4},{6,7},{7,6},{8,9},{9,8},{10,11... | collective-permute-start | bytes 196616 | tf_op jit(solution)/shard_map/ppermute | solution.py:454
  94.7 8.7 %collective-permute-start.10 = (bf16[128,256]{1,0:T(8,128)(2,1)S(1)}, bf16[128,256]{1,0:T(8,128)(2,1)S(1)}, u32[]{:S(2)}, u32[]{:S(2)}) collective-permute-start(bf16[128,256]{1,0:T(8,128)(2,1)S(1)} %collective-permute-done.9.refs_7_), channel_id=1, source_target_pairs={{0,1},{1,0},{2,3},{3,2},{4,5},{5,4},{6,7},{7,6},{8,9},{9,8},{10,11... | collective-permute-start | bytes 196616 | tf_op jit(solution)/shard_map/ppermute | solution.py:454
  94.9 8.5 %collective-permute-start.6 = (bf16[128,256]{1,0:T(8,128)(2,1)S(1)}, bf16[128,256]{1,0:T(8,128)(2,1)S(1)}, u32[]{:S(2)}, u32[]{:S(2)}) collective-permute-start(bf16[128,256]{1,0:T(8,128)(2,1)S(1)} %collective-permute-done.5.refs_5_), channel_id=1, source_target_pairs={{0,1},{1,0},{2,3},{3,2},{4,5},{5,4},{6,7},{7,6},{8,9},{9,8},{10,11... | collective-permute-start | bytes 196616 | tf_op jit(solution)/shard_map/ppermute | solution.py:454
  98.0 5.9 %collective-permute-start.16 = (bf16[128,256]{1,0:T(8,128)(2,1)S(1)}, bf16[128,256]{1,0:T(8,128)(2,1)S(1)}, u32[]{:S(2)}, u32[]{:S(2)}) collective-permute-start(bf16[128,256]{1,0:T(8,128)(2,1)S(1)} %row_sum.3.refs_12_), channel_id=1, source_target_pairs={{0,2},{1,3},{2,0},{3,1},{4,6},{5,7},{6,4},{7,5},{8,10},{9,11},{10,... | collective-permute-start | bytes 196616 | tf_op jit(solution)/shard_map/ppermute | solution.py:454
  101.6 7.9 %collective-permute-start.18 = (bf16[128,256]{1,0:T(8,128)(2,1)S(1)}, bf16[128,256]{1,0:T(8,128)(2,1)S(1)}, u32[]{:S(2)}, u32[]{:S(2)}) collective-permute-start(bf16[128,256]{1,0:T(8,128)(2,1)S(1)} %row_sum.3.refs_12_), channel_id=1, source_target_pairs={{0,4},{1,5},{2,6},{3,7},{4,0},{5,1},{6,2},{7,3},{8,12},{9,13},{10,... | collective-permute-start | bytes 196616 | tf_op jit(solution)/shard_map/ppermute | solution.py:454
  102.7 6.8 %collective-permute-start.20 = (bf16[128,256]{1,0:T(8,128)(2,1)S(1)}, bf16[128,256]{1,0:T(8,128)(2,1)S(1)}, u32[]{:S(2)}, u32[]{:S(2)}) collective-permute-start(bf16[128,256]{1,0:T(8,128)(2,1)S(1)} %row_sum.3.refs_12_), channel_id=1, source_target_pairs={{0,6},{1,7},{2,4},{3,5},{4,2},{5,3},{6,0},{7,1},{8,14},{9,15},{10,... | collective-permute-start | bytes 196616 | tf_op jit(solution)/shard_map/ppermute | solution.py:454
  103.4 6.6 %collective-permute-start.8 = (bf16[128,256]{1,0:T(8,128)(2,1)S(1)}, bf16[128,256]{1,0:T(8,128)(2,1)S(1)}, u32[]{:S(2)}, u32[]{:S(2)}) collective-permute-start(bf16[128,256]{1,0:T(8,128)(2,1)S(1)} %collective-permute-done.7.refs_6_), channel_id=1, source_target_pairs={{0,1},{1,0},{2,3},{3,2},{4,5},{5,4},{6,7},{7,6},{8,9},{9,8},{10,11... | collective-permute-start | bytes 196616 | tf_op jit(solution)/shard_map/ppermute | solution.py:454
  103.4 6.6 %collective-permute-start.15 = (bf16[128,256]{1,0:T(8,128)(2,1)S(1)}, bf16[128,256]{1,0:T(8,128)(2,1)S(1)}, u32[]{:S(2)}, u32[]{:S(2)}) collective-permute-start(bf16[128,256]{1,0:T(8,128)(2,1)S(1)} %row_sum.3.refs_12_), channel_id=1, source_target_pairs={{0,1},{1,0},{2,3},{3,2},{4,5},{5,4},{6,7},{7,6},{8,9},{9,8},{10,11... | collective-permute-start | bytes 196616 | tf_op jit(solution)/shard_map/ppermute | solution.py:454
  104.0 6.1 %collective-permute-start.17 = (bf16[128,256]{1,0:T(8,128)(2,1)S(1)}, bf16[128,256]{1,0:T(8,128)(2,1)S(1)}, u32[]{:S(2)}, u32[]{:S(2)}) collective-permute-start(bf16[128,256]{1,0:T(8,128)(2,1)S(1)} %collective-permute-done.16.refs_13_), channel_id=1, source_target_pairs={{0,1},{1,0},{2,3},{3,2},{4,5},{5,4},{6,7},{7,6},{8,9},{9,8},{10,11... | collective-permute-start | bytes 196616 | tf_op jit(solution)/shard_map/ppermute | solution.py:454
  109.5 1.3 collective-permute-start.19
  109.5 1.4 %collective-permute-start.21 = (bf16[128,256]{1,0:T(8,128)(2,1)S(1)}, bf16[128,256]{1,0:T(8,128)(2,1)S(1)}, u32[]{:S(2)}, u32[]{:S(2)}) collective-permute-start(bf16[128,256]{1,0:T(8,128)(2,1)S(1)} %collective-permute-done.20.refs_15_), channel_id=1, source_target_pairs={{0,1},{1,0},{2,3},{3,2},{4,5},{5,4},{6,7},{7,6},{8,9},{9,8},{10,11... | collective-permute-start | bytes 196616 | tf_op jit(solution)/shard_map/ppermute | solution.py:454
